TPU v7x, 256 devices: a whole 4x4x8 slice. The times are simulated.
256 devices in a mesh: gx: 16 (over z, core), gy: 8 (over x, y_lo), seq: 2 (over y_hi).
Axes of the slice: x: 4, y: 4 (y_hi: 2, y_lo: 2; y = y_hi * 2 + y_lo), z: 8, core: 2. Of those that a mesh axis runs over, the one named last changes fastest.
Arguments:
- queries: bfloat16 [32, 64, 16, 1024], P('gx', 'gy', 'seq'), may hold values from -6 to 6
- keys: bfloat16 [2048, 1024], P(('gx', 'gy', 'seq')), may hold values from -8 to 8
- values: bfloat16 [2048, 1024], P(('gx', 'gy', 'seq')), may hold values from -6 to 6
- w_out: bfloat16 [1024, 256], replicated, may hold values from -0.1875 to 0.1875
- conv_first: bfloat16 [3, 3, 3, 256, 128], replicated, may hold values from -0.078125 to 0.078125
- conv_second: bfloat16 [3, 3, 3, 128, 128], replicated, may hold values from -0.109375 to 0.109375
Outputs:
- decoded: bfloat16 [64, 128, 32, 128], P('gx', 'gy', 'seq')
All inputs are finite; a program needn't handle non-finite values.
Results may differ from a plain program's by a relative error of at most 0.02.
Values may be sent and summed in bfloat16 or wider, within the bound.
No kernel may reach another device: no remote copies, remote signals or barrier semaphores. Data moves between devices by JAX's collectives and lax.ppermute only.
A program may use at most 64 MiB of HBM per device.

v0:
```python
import jax
import jax.numpy as jnp
from jax import lax
from jax.sharding import PartitionSpec as P

H = 8


def with_halo(cells, sides, width):
    for axis, dim in sides:
        count = lax.axis_size(axis)
        ends = count - 1
        head = lax.slice_in_dim(cells, 0, width, axis=dim)
        tail = lax.slice_in_dim(cells, cells.shape[dim] - width, cells.shape[dim], axis=dim)
        cells = jnp.concatenate(
            [
                lax.ppermute(tail, axis, [(i, (i + 1) % count) for i in range(ends)]),
                cells,
                lax.ppermute(head, axis, [((i + 1) % count, i) for i in range(ends)]),
            ],
            axis=dim,
        )
    return cells


def conv_layer(padded, weight, size_x, size_y, size_z):
    cin = weight.shape[3]
    cout = weight.shape[4]
    total = jnp.zeros((size_x * size_y * size_z, cout), jnp.float32)
    for a in range(3):
        for b in range(3):
            stacked = jnp.concatenate(
                [padded[a : a + size_x, b : b + size_y, c : c + size_z] for c in range(3)], axis=-1
            )
            stacked = stacked.reshape(-1, 3 * cin)
            total = total + jnp.dot(
                stacked, weight[a, b].reshape(3 * cin, cout), preferred_element_type=jnp.float32
            )
    return total.reshape(size_x, size_y, size_z, cout)


def upsample(field):
    return jnp.repeat(jnp.repeat(jnp.repeat(field, 2, axis=0), 2, axis=1), 2, axis=2)


def head_scores(rows, key_rows, head, head_size):
    query_part = rows[:, head * head_size : (head + 1) * head_size]
    key_part = key_rows[:, head * head_size : (head + 1) * head_size]
    scores = lax.dot_general(
        query_part, key_part, (((1,), (1,)), ((), ())), preferred_element_type=jnp.float32
    )
    return scores * head_size ** (-0.5)


def full_attention(rows, key_rows, value_rows, heads, head_size):
    outputs = []
    for head in range(heads):
        scores = head_scores(rows, key_rows, head, head_size)
        top = jnp.max(scores, axis=1, keepdims=True)
        weights = jnp.exp(scores - top).astype(jnp.bfloat16)
        total = jnp.sum(weights.astype(jnp.float32), axis=1, keepdims=True)
        summed = jnp.dot(
            weights,
            value_rows[:, head * head_size : (head + 1) * head_size],
            preferred_element_type=jnp.float32,
        )
        outputs.append(summed / total)
    return jnp.concatenate(outputs, axis=1).astype(jnp.bfloat16)


def body(queries, keys, values, w_out, conv_first, conv_second):
    size_x, size_y, size_z, width = queries.shape
    heads = H
    head_size = width // heads
    rows = queries.reshape(-1, width)
    key_rows, value_rows = (
        lax.all_gather(keys, ("gx", "gy", "seq"), axis=0, tiled=True),
        lax.all_gather(values, ("gx", "gy", "seq"), axis=0, tiled=True),
    )
    attended = full_attention(rows, key_rows, value_rows, heads, head_size)
    projected = jnp.dot(attended, w_out, preferred_element_type=jnp.float32)
    normed = projected * lax.rsqrt(jnp.mean(projected * projected, axis=-1, keepdims=True) + 1e-06)
    normed = normed.astype(jnp.bfloat16).reshape(size_x, size_y, size_z, w_out.shape[1])
    padded = with_halo(normed, (("gx", 0), ("gy", 1), ("seq", 2)), 1)
    first = conv_layer(padded, conv_first, size_x, size_y, size_z)
    hidden = jax.nn.silu(first).astype(jnp.bfloat16)
    upsampled = upsample(hidden)
    padded_up = with_halo(upsampled, (("gx", 0), ("gy", 1), ("seq", 2)), 1)
    second = conv_layer(padded_up, conv_second, 2 * size_x, 2 * size_y, 2 * size_z)
    return second.astype(jnp.bfloat16)


def solution(mesh):
    in_specs = (
        P("gx", "gy", "seq", None),
        P(("gx", "gy", "seq"), None),
        P(("gx", "gy", "seq"), None),
        P(),
        P(),
        P(),
    )
    out_specs = P("gx", "gy", "seq", None)
    return jax.shard_map(body, mesh=mesh, in_specs=in_specs, out_specs=out_specs, check_vma=False)
```

profile of v0, /device:TPU:97, one launch (start us, length us, event | category | flops | bytes accessed | tf_op | source)
XLA Modules:
  0.0 1512.3 jit_solution(7745640340206660496)
XLA Ops:
  6.5 0.7 all-gather.3.cloned.1.call-update
  8.0 712.1 %all-gather.3.cloned.1.call-done = bf16[2048,1024]{1,0:T(8,128)(2,1)} async-done(((bf16[8,1024]{1,0:T(8,128)(2,1)}), bf16[2048,1024]{1,0:T(8,128)(2,1)}) %all-gather.3.cloned.1.call-update) | async-done | bytes 4194320 | tf_op jit(solution)/shard_map/all_gather | solution.py:77
  720.1 1.6 fusion.71
  722.0 1.4 fusion.72
  728.3 700.2 %all-gather.5.cloned.1.call-done = bf16[2048,1024]{1,0:T(8,128)(2,1)} async-done(((bf16[8,1024]{1,0:T(8,128)(2,1)}), bf16[2048,1024]{1,0:T(8,128)(2,1)}) %all-gather.5.cloned.1.call-update) | async-done | bytes 4194320 | tf_op jit(solution)/shard_map/all_gather | solution.py:78
  1428.5 1.5 fusion.2
  1430.1 1.5 fusion.4
  1431.6 1.5 fusion.6
  1433.2 1.5 fusion.8
  1434.7 1.5 fusion.10
  1436.2 1.4 fusion.12
  1437.7 1.4 fusion.14
  1439.1 1.6 fusion.16
  1441.1 4.5 collective-permute-start
  1445.6 2.5 collective-permute-start.1
  1448.1 4.0 collective-permute-done.1
  1452.1 1.3 collective-permute-start.2
  1453.4 1.3 collective-permute-start.3
  1454.9 5.2 collective-permute-done.3
  1460.1 1.3 collective-permute-start.4
  1461.4 1.3 collective-permute-start.5
  1462.8 4.9 collective-permute-done.5
  1470.1 4.2 collective-permute-start.6
  1474.4 1.9 collective-permute-start.7
  1476.3 4.9 collective-permute-done.7
  1481.4 4.5 collective-permute-start.8
  1485.9 1.3 collective-permute-start.9
  1487.3 3.2 collective-permute-done.9
  1490.8 1.9 collective-permute-start.10
  1492.8 1.5 collective-permute-start.11
  1494.4 4.8 collective-permute-done.11
  1504.4 1.1 fusion
  (117 shorter events, 14.7 us)
Async XLA Ops:
  6.5 1434.1 %copy-start = (bf16[1024,256]{1,0:T(8,128)(2,1)S(1)}, bf16[1024,256]{1,0:T(8,128)(2,1)}, u32[]{:S(2)}) copy-start(bf16[1024,256]{1,0:T(8,128)(2,1)} %param.9) | copy-start | bytes 1572868
  6.5 715.5 %copy-start.16 = (bf16[2,8,8,1024]{3,2,1,0:T(8,128)(2,1)S(1)}, bf16[2,8,8,1024]{3,2,1,0:T(8,128)(2,1)}, u32[]{:S(2)}) copy-start(bf16[2,8,8,1024]{3,2,1,0:T(8,128)(2,1)} %param.6) | copy-start | bytes 786436
  6.5 713.6 %all-gather.3.cloned.1.call-start = ((), (), s32[]{:S(2)}) async-start(), calls=%async_computation | async-start | bytes 4210688 | tf_op jit(solution)/shard_map/all_gather | solution.py:77
  7.3 1421.3 %all-gather.5.cloned.1.call-start = ((), (), s32[]{:S(2)}) async-start(), calls=%async_computation.1 | async-start | bytes 4210688 | tf_op jit(solution)/shard_map/all_gather | solution.py:78
  720.1 3.6 copy-start.1
  723.4 1.1 copy-start.2
  724.2 1.1 copy-start.4
  724.9 1.0 copy-start.6
  725.6 1.0 copy-start.8
  726.4 1.0 copy-start.10
  727.1 1.0 copy-start.12
  1428.5 1.6 copy-start.3
  1428.5 3.1 copy-start.5
  1430.1 3.1 copy-start.7
  1431.6 3.1 copy-start.9
  1433.2 3.1 copy-start.11
  1434.7 3.0 copy-start.13
  1439.1 15.6 %copy-start.14 = (bf16[3,3,3,256,128]{4,3,2,1,0:T(8,128)(2,1)S(1)}, bf16[3,3,3,256,128]{4,3,2,1,0:T(8,128)(2,1)}, u32[]{:S(2)}) copy-start(bf16[3,3,3,256,128]{4,3,2,1,0:T(8,128)(2,1)} %param.10) | copy-start | bytes 5308420
  1441.1 7.0 collective-permute-start
  1445.6 6.4 collective-permute-start.1
  1452.1 2.8 collective-permute-start.2
  1453.4 6.7 collective-permute-start.3
  1460.1 2.7 collective-permute-start.4
  1461.4 6.3 collective-permute-start.5
  1469.4 17.9 %copy-start.15 = (bf16[3,3,3,128,128]{4,3,2,1,0:T(8,128)(2,1)S(1)}, bf16[3,3,3,128,128]{4,3,2,1,0:T(8,128)(2,1)}, u32[]{:S(2)}) copy-start(bf16[3,3,3,128,128]{4,3,2,1,0:T(8,128)(2,1)} %param.11) | copy-start | bytes 2654212
  1470.1 6.2 collective-permute-start.6
  1474.4 6.8 collective-permute-start.7
  1481.4 5.9 collective-permute-start.8
  1485.9 4.6 collective-permute-start.9
  1490.8 3.6 collective-permute-start.10
  1492.8 6.4 collective-permute-start.11
Sparse Core Ops, SparseCore 0:
  9.2 710.8 all-gather.2
  722.0 706.4 all-gather.4
where the time goes:
time: 1510 us
  waiting for transfers between devices  1440 us (95%)
  starting transfers between devices  27.6 us (2%)
  matrix products  23.6 us (2%)
    all_gather x1, waiting for transfers between devices, body(): lax.all_gather(keys, ('gx', 'gy', 'seq'), axis=0, tiled=True)  712 us
    all_gather x1, waiting for transfers between devices, body(): lax.all_gather(values, ('gx', 'gy', 'seq'), axis=0, tiled=True)  700 us
  transfers between devices with their start and end apart: 14, of which 8 were waited for; matrix products, arithmetic and copies ran while one was open for 1% of the time, Pallas kernels for 0%

commit v1 on v0

--- a/solution.py
+++ b/solution.py
@@ -74,7 +74,12 @@
     head_size = width // heads
     rows = queries.reshape(-1, width)
     key_rows, value_rows = (
-        lax.all_gather(keys, ("gx", "gy", "seq"), axis=0, tiled=True),
+        jnp.concatenate(
+            lax.all_to_all(
+                jnp.stack([keys] * lax.axis_size(("gx", "gy", "seq"))), ("gx", "gy", "seq"), 0, 0
+            ),
+            axis=0,
+        ),
         lax.all_gather(values, ("gx", "gy", "seq"), axis=0, tiled=True),
     )
     attended = full_attention(rows, key_rows, value_rows, heads, head_size)

time: 1510 us -> 837 us (0.55)
  waiting for transfers between devices: 1440 us -> 741 us
    all_gather x1 -> x0, waiting for transfers between devices: 712 us -> none  [body(): lax.all_gather(keys, ('gx', 'gy', 'seq'), axis=0, tiled=True)]
    all_to_all x0 -> x1, waiting for transfers between devices: none -> 93 us  [body(): lax.all_to_all(jnp.stack([keys] * lax.axis_size(('gx', 'gy', 'seq'))), ('...]
    all_gather x1, waiting for transfers between devices: 700 us -> 620 us  [body(): lax.all_gather(values, ('gx', 'gy', 'seq'), axis=0, tiled=True)]
    all_to_all x0 -> x1, starting transfers between devices: none -> 15.3 us  [body(): lax.all_to_all(jnp.stack([keys] * lax.axis_size(('gx', 'gy', 'seq'))), ('...]
  transfers between devices with their start and end apart: 14 -> 14, of which waited for: 8 -> 8; matrix products, arithmetic and copies ran while one was open for 1% -> 2% of each run, Pallas kernels for 0% -> 0%
where the time goes in v1:
time: 837 us; the launch traced here: 836 us
  waiting for transfers between devices  741 us (89%)
  starting transfers between devices  41.8 us (5%)
  matrix products  29.9 us (4%)
  between operations  14.2 us (2%)
    all_gather x1, waiting for transfers between devices, body(): lax.all_gather(values, ('gx', 'gy', 'seq'), axis=0, tiled=True)  620 us
    all_to_all x1, waiting for transfers between devices, body(): lax.all_to_all(jnp.stack([keys] * lax.axis_size(('gx', 'gy', 'seq'))), ('...  93 us
    ppermute x6, waiting for transfers between devices, with_halo(): lax.ppermute(head, axis, [((i + 1) % count, i) for i in range(ends)])  27.1 us
  transfers between devices with their start and end apart: 14, of which 8 were waited for; matrix products, arithmetic and copies ran while one was open for 2% of the time, Pallas kernels for 0%

profile of v1, /device:TPU:97, one launch (start us, length us, event | category | flops | bytes accessed | tf_op | source)
XLA Modules:
  0.0 836.5 jit_solution(18147735027182744413)
XLA Ops:
  6.5 3.3 stack.2
  9.8 15.3 %all-to-all-start = ((bf16[256,8,1024]{2,1,0:T(8,128)(2,1)}), bf16[256,8,1024]{2,1,0:T(8,128)(2,1)}, u32[]{:S(2)}, u32[]{:S(2)}) async-start(bf16[256,8,1024]{2,1,0:T(8,128)(2,1)} %stack.2), calls=%async_computation | async-start | bytes 8388608 | tf_op jit(solution)/shard_map/all_to_all | solution.py:78
  25.9 93.0 %all-to-all-done = bf16[256,8,1024]{2,1,0:T(8,128)(2,1)} async-done(((bf16[256,8,1024]{2,1,0:T(8,128)(2,1)}), bf16[256,8,1024]{2,1,0:T(8,128)(2,1)}, u32[]{:S(2)}, u32[]{:S(2)}) %all-to-all-start) | async-done | bytes 4194336 | tf_op jit(solution)/shard_map/all_to_all | solution.py:78
  120.6 1.4 fusion.72
  122.3 1.5 fusion.73
  124.1 1.5 fusion.74
  125.9 1.5 fusion.75
  127.7 1.5 fusion.76
  129.5 1.5 fusion.77
  131.3 1.5 fusion.78
  133.1 620.4 %all-gather.2.cloned.1.call-done = bf16[2048,1024]{1,0:T(8,128)(2,1)} async-done(((bf16[8,1024]{1,0:T(8,128)(2,1)}), bf16[2048,1024]{1,0:T(8,128)(2,1)}) %all-gather.2.cloned.1.call-update) | async-done | bytes 4194320 | tf_op jit(solution)/shard_map/all_gather | solution.py:83
  753.5 1.5 fusion.2
  755.1 1.5 fusion.4
  756.6 1.5 fusion.6
  758.2 1.5 fusion.8
  759.7 1.5 fusion.10
  761.2 1.4 fusion.12
  762.7 1.4 fusion.14
  764.1 1.6 fusion.16
  766.1 3.4 collective-permute-start
  769.5 2.5 collective-permute-start.1
  772.0 4.0 collective-permute-done.1
  778.8 5.5 collective-permute-done.3
  787.0 4.9 collective-permute-done.5
  794.3 4.2 collective-permute-start.6
  798.6 1.9 collective-permute-start.7
  800.5 4.9 collective-permute-done.7
  805.6 4.5 collective-permute-start.8
  811.5 3.2 collective-permute-done.9
  815.0 1.9 collective-permute-start.10
  817.0 1.5 collective-permute-start.11
  818.6 4.8 collective-permute-done.11
  (115 shorter events, 20.9 us)
Async XLA Ops:
  6.5 759.1 %copy-start = (bf16[1024,256]{1,0:T(8,128)(2,1)S(1)}, bf16[1024,256]{1,0:T(8,128)(2,1)}, u32[]{:S(2)}) copy-start(bf16[1024,256]{1,0:T(8,128)(2,1)} %param.9) | copy-start | bytes 1572868
  9.8 109.0 %copy-start.15 = (bf16[2,8,8,1024]{3,2,1,0:T(8,128)(2,1)S(1)}, bf16[2,8,8,1024]{3,2,1,0:T(8,128)(2,1)}, u32[]{:S(2)}) copy-start(bf16[2,8,8,1024]{3,2,1,0:T(8,128)(2,1)} %param.6) | copy-start | bytes 786436
  9.8 109.0 %all-to-all-start = ((bf16[256,8,1024]{2,1,0:T(8,128)(2,1)}), bf16[256,8,1024]{2,1,0:T(8,128)(2,1)}, u32[]{:S(2)}, u32[]{:S(2)}) async-start(bf16[256,8,1024]{2,1,0:T(8,128)(2,1)} %stack.2), calls=%async_computation | async-start | bytes 8388608 | tf_op jit(solution)/shard_map/all_to_all | solution.py:78
  25.1 728.4 %all-gather.2.cloned.1.call-start = ((), (), s32[]{:S(2)}) async-start(), calls=%async_computation.1 | async-start | bytes 4210688 | tf_op jit(solution)/shard_map/all_gather | solution.py:83
  122.0 2.1 copy-start.1
  123.8 2.1 copy-start.3
  125.6 2.1 copy-start.5
  127.4 2.1 copy-start.7
  129.2 2.1 copy-start.9
  131.0 1.8 copy-start.11
  753.5 1.6 copy-start.2
  753.5 3.1 copy-start.4
  755.1 3.1 copy-start.6
  756.6 3.1 copy-start.8
  758.2 3.1 copy-start.10
  759.7 3.0 copy-start.12
  764.1 14.5 %copy-start.13 = (bf16[3,3,3,256,128]{4,3,2,1,0:T(8,128)(2,1)S(1)}, bf16[3,3,3,256,128]{4,3,2,1,0:T(8,128)(2,1)}, u32[]{:S(2)}) copy-start(bf16[3,3,3,256,128]{4,3,2,1,0:T(8,128)(2,1)} %param.10) | copy-start | bytes 5308420
  766.1 5.9 collective-permute-start
  769.5 6.4 collective-permute-start.1
  776.0 2.8 collective-permute-start.2
  777.3 7.0 collective-permute-start.3
  784.3 2.7 collective-permute-start.4
  785.6 6.3 collective-permute-start.5
  793.6 17.9 %copy-start.14 = (bf16[3,3,3,128,128]{4,3,2,1,0:T(8,128)(2,1)S(1)}, bf16[3,3,3,128,128]{4,3,2,1,0:T(8,128)(2,1)}, u32[]{:S(2)}) copy-start(bf16[3,3,3,128,128]{4,3,2,1,0:T(8,128)(2,1)} %param.11) | copy-start | bytes 2654212
  794.3 6.2 collective-permute-start.6
  798.6 6.8 collective-permute-start.7
  805.6 5.9 collective-permute-start.8
  810.1 4.6 collective-permute-start.9
  815.0 3.6 collective-permute-start.10
  817.0 6.4 collective-permute-start.11
Sparse Core Ops, SparseCore 0:
  27.9 725.6 all-gather.1
